TPU v7x, 32 devices: a whole 2x2x4 slice. The times are simulated.
32 devices in a mesh: gx: 8 (over z, x), gy: 4 (over y, core).
Axes of the slice: x: 2, y: 2, z: 4, core: 2. Of those that a mesh axis runs over, the one named last changes fastest.
Arguments:
- volume: float32 [64, 16, 32, 128], P(None, 'gx', 'gy'), may hold values from -6 to 6
- cotangent: float32 [64, 16, 32, 128], P(None, 'gx', 'gy'), may hold values from -20 to 20
- weight_one: float32 [27, 4096], replicated, may hold values from -0.17 to 0.16, as said below
- scale_one: float32 [64], replicated, may hold values from 0.001 to 0.016
- weight_two: float32 [27, 4096], replicated, may hold values from -0.17 to 0.16, as said below
- scale_two: float32 [64], replicated, may hold values from 0.001 to 0.016
Outputs:
- input_grad: float32 [64, 16, 32, 128], P(None, 'gx', 'gy')
- kernel_grad_one: float32 [27, 4096], P(None, ('gx', 'gy'))
- scale_grad_one: float32 [64], replicated
- kernel_grad_two: float32 [27, 4096], P(None, ('gx', 'gy'))
- scale_grad_two: float32 [64], replicated
Inputs may be any that keep to these rules, and one draw needn't show every extreme that they name: `weight_one`: each entry divided by its output channel's entry of scale_one lies 0.1 to 0.4 away from the nearest integer, between -10.4 and 9.4. `weight_two`: each entry divided by its output channel's entry of scale_two lies 0.1 to 0.4 away from the nearest integer, between -10.4 and 9.4.
All inputs are finite; a program needn't handle non-finite values.
Results may differ from a plain program's by a relative error of at most 0.0003.
Values sent between devices are 32-bit elements; how exact they have to be, the bound alone decides.
A program may use at most 128 MiB of HBM per device.

v0:
```python
import functools

import jax
import jax.numpy as jnp
from jax import lax
from jax.experimental import pallas as pl
from jax.experimental.pallas import tpu as pltpu
from jax.sharding import PartitionSpec as P

CODE_LOW = -8.0
CODE_HIGH = 7.0
REPORT = 2.0 ** (-10)
WAYS = [(dx, dy) for dx in (-1, 0, 1) for dy in (-1, 0, 1) if (dx, dy) != (0, 0)]


def quantize(weight, scales):
    channels = scales.shape[0]
    ratios = weight.reshape(27, channels, channels) / scales[None, :, None]
    levels = jnp.clip(jnp.floor(ratios + 0.5), CODE_LOW, CODE_HIGH)
    inside = jnp.logical_and(ratios >= CODE_LOW, ratios <= CODE_HIGH)
    residue = jnp.where(inside, levels - ratios, levels)
    return (levels, inside, residue)


def forward_matrix(levels):
    ch = levels.shape[1]
    taps = levels.astype(jnp.bfloat16).reshape(3, 3, 3, ch, ch).transpose(0, 2, 3, 1, 4)
    taps = jnp.broadcast_to(taps[:, :, :, :, None, :], (3, 3, ch, 3, 2, ch))
    return taps.reshape(3, 3 * ch, 6 * ch)


def backward_matrix(levels):
    ch = levels.shape[1]
    taps = jnp.flip(levels.astype(jnp.bfloat16).reshape(3, 3, 3, ch, ch), (0, 1, 2))
    taps = taps.transpose(0, 2, 4, 1, 3)
    taps = jnp.broadcast_to(taps[:, :, :, :, None, :], (3, 3, ch, 3, 2, ch))
    return taps.reshape(3, 3 * ch, 6 * ch)


def halves(value):
    high = value.astype(jnp.bfloat16)
    low = (value - high.astype(jnp.float32)).astype(jnp.bfloat16)
    return high, low


def kernel(
    sizes, vol, cot, s1, s2, f1, f2, b2, b1, out, g1, g2,
    pad0, pad1, pad2, pad3, vol_h, hid_h, del_h, stage, slope, send_sem, recv_sem,
):
    nx, ny, ch, width = vol.shape
    size_x, size_y = sizes
    me_x, me_y = lax.axis_index("gx"), lax.axis_index("gy")
    rows = nx * ny
    lane = lax.broadcasted_iota(jnp.int32, (ch, width), 1)

    for pad in (pad0, pad1, pad2, pad3):
        pad[...] = jnp.zeros_like(pad)
    g1[...] = jnp.zeros_like(g1)
    g2[...] = jnp.zeros_like(g2)

    def there(dx, dy):
        x, y = me_x + dx, me_y + dy
        return (x >= 0) & (x < size_x) & (y >= 0) & (y < size_y)

    barrier = pltpu.get_barrier_semaphore()
    count = jnp.int32(0)
    for dx, dy in WAYS:
        valid = there(dx, dy)
        count = count + jnp.where(valid, 1, 0)

        @pl.when(valid)
        def _(dx=dx, dy=dy):
            pl.semaphore_signal(
                barrier, inc=1, device_id=(me_x + dx, me_y + dy),
                device_id_type=pl.DeviceIdType.MESH,
            )

    pl.semaphore_wait(barrier, count)

    def spans(step, length):
        if step == 1:
            return pl.ds(length, 1), pl.ds(0, 1)
        if step == -1:
            return pl.ds(1, 1), pl.ds(length + 1, 1)
        return pl.ds(1, length), pl.ds(1, length)

    def remote(pad, turn, way, dx, dy):
        from_x, to_x = spans(dx, nx)
        from_y, to_y = spans(dy, ny)
        return pltpu.make_async_remote_copy(
            src_ref=pad.at[from_x, from_y],
            dst_ref=pad.at[to_x, to_y],
            send_sem=send_sem.at[turn, way],
            recv_sem=recv_sem.at[turn, way],
            device_id=(me_x + dx, me_y + dy),
            device_id_type=pl.DeviceIdType.MESH,
        )

    def send(pad, turn):
        for way, (dx, dy) in enumerate(WAYS):
            @pl.when(there(dx, dy))
            def _(way=way, dx=dx, dy=dy):
                remote(pad, turn, way, dx, dy).start()

    def receive(pad, turn):
        for way, (dx, dy) in enumerate(WAYS):
            @pl.when(there(-dx, -dy))
            def _(way=way, dx=dx, dy=dy):
                remote(pad, turn, way, dx, dy).wait_recv()

    def sent(pad, turn):
        for way, (dx, dy) in enumerate(WAYS):
            @pl.when(there(dx, dy))
            def _(way=way, dx=dx, dy=dy):
                remote(pad, turn, way, dx, dy).wait_send()

    def split(pad, target):
        for x in range(nx + 2):
            def body(y, carry, x=x):
                high, low = halves(pad[x, y])
                target[x, y, 0:ch, :] = high
                target[x, y, ch:2 * ch, :] = low
                return carry

            lax.fori_loop(0, ny + 2, body, 0)

    def conv_row(source, matrix, x, y):
        total = None
        for a in range(3):
            block = source[x + a, pl.ds(y, 3)].reshape(6 * ch, width)
            part = jnp.dot(matrix[a], block, preferred_element_type=jnp.float32)
            total = part if total is None else total + part
        before = jnp.where(lane == 0, 0.0, pltpu.roll(total[0:ch], 1, 1))
        after = jnp.where(lane == width - 1, 0.0, pltpu.roll(total[2 * ch:3 * ch], width - 1, 1))
        return before + total[ch:2 * ch] + after

    def grad_row(delta, source, target, x, y):
        left = jnp.where(lane == width - 1, 0.0, pltpu.roll(delta, width - 1, 1))
        right = jnp.where(lane == 0, 0.0, pltpu.roll(delta, 1, 1))
        parts = []
        for shifted in (left, delta, right):
            parts.extend(halves(shifted))
        stack = jnp.concatenate(parts, axis=0)
        for a in range(3):
            block = source[x + a, pl.ds(y, 3)].reshape(6 * ch, width)
            prod = lax.dot_general(
                stack, block, (((1,), (1,)), ((), ())), preferred_element_type=jnp.float32
            )
            for c in range(3):
                first = prod[2 * c * ch:(2 * c + 1) * ch]
                second = prod[(2 * c + 1) * ch:(2 * c + 2) * ch]
                target[a, c * ch:(c + 1) * ch, :] += first + second

    def each_row(body):
        for x in range(nx):
            def step(y, carry, x=x):
                body(x, y)
                return carry

            lax.fori_loop(0, ny, step, 0)

    pad0[1:nx + 1, 1:ny + 1] = vol[...]
    send(pad0, 0)
    receive(pad0, 0)
    split(pad0, vol_h)

    def first(x, y):
        pre = conv_row(vol_h, f1, x, y) * s1[...]
        sig = 1.0 / (1.0 + jnp.exp(-pre))
        stage[x, y] = pre * sig
        slope[x, y] = sig * (1.0 + pre * (1.0 - sig))

    each_row(first)

    pad1[1:nx + 1, 1:ny + 1] = stage[...]
    send(pad1, 1)
    receive(pad1, 1)
    split(pad1, hid_h)

    def second(x, y):
        pre = conv_row(hid_h, f2, x, y) * s2[...]
        sig = 1.0 / (1.0 + jnp.exp(-pre))
        stage[x, y] = cot[x, y] * (sig * (1.0 + pre * (1.0 - sig)))

    each_row(second)

    pad2[1:nx + 1, 1:ny + 1] = stage[...] * s2[...]
    send(pad2, 2)
    each_row(lambda x, y: grad_row(stage[x, y], hid_h, g2, x, y))
    receive(pad2, 2)
    split(pad2, del_h)

    def third(x, y):
        stage[x, y] = conv_row(del_h, b2, x, y) * slope[x, y]

    each_row(third)

    pad3[1:nx + 1, 1:ny + 1] = stage[...] * s1[...]
    send(pad3, 3)
    each_row(lambda x, y: grad_row(stage[x, y], vol_h, g1, x, y))
    receive(pad3, 3)
    split(pad3, del_h)

    def fourth(x, y):
        out[x, y] = conv_row(del_h, b1, x, y)

    each_row(fourth)
    for turn, pad in enumerate((pad0, pad1, pad2, pad3)):
        sent(pad, turn)


def gradient(raw, channels):
    taps = raw.reshape(3, 3, channels, 3, 2, channels).sum(axis=4)
    return taps.transpose(0, 3, 1, 2, 4).reshape(27, channels, channels)


def on_device(volume, cotangent, weight_one, scale_one, weight_two, scale_two):
    channels = scale_one.shape[0]
    ch, nx, ny, width = volume.shape
    sizes = (lax.axis_size("gx"), lax.axis_size("gy"))
    level_one, inside_one, residue_one = quantize(weight_one, scale_one)
    level_two, inside_two, residue_two = quantize(weight_two, scale_two)
    vmem = pl.BlockSpec(memory_space=pltpu.VMEM)
    cells = jax.ShapeDtypeStruct((nx, ny, ch, width), jnp.float32)
    grads = jax.ShapeDtypeStruct((3, 3 * ch, 6 * ch), jnp.float32)
    pad = pltpu.VMEM((nx + 2, ny + 2, ch, width), jnp.float32)
    half = pltpu.VMEM((nx + 2, ny + 2, 2 * ch, width), jnp.bfloat16)
    local = pltpu.VMEM((nx, ny, ch, width), jnp.float32)
    moved, raw_one, raw_two = pl.pallas_call(
        functools.partial(kernel, sizes),
        out_shape=(cells, grads, grads),
        in_specs=[vmem] * 8,
        out_specs=(vmem, vmem, vmem),
        scratch_shapes=[
            pad, pad, pad, pad, half, half, half, local, local,
            pltpu.SemaphoreType.DMA((4, 8)),
            pltpu.SemaphoreType.DMA((4, 8)),
        ],
        compiler_params=pltpu.CompilerParams(
            collective_id=0, has_side_effects=True, vmem_limit_bytes=48 * 2 ** 20
        ),
    )(
        volume.transpose(1, 2, 0, 3),
        cotangent.transpose(1, 2, 0, 3),
        jnp.broadcast_to(scale_one[:, None], (ch, width)),
        jnp.broadcast_to(scale_two[:, None], (ch, width)),
        forward_matrix(level_one),
        forward_matrix(level_two),
        backward_matrix(level_two),
        backward_matrix(level_one),
    )
    input_grad = moved.transpose(2, 0, 1, 3)
    devices = sizes[0] * sizes[1]
    share = channels * channels // devices
    factor = REPORT * (27.0 * channels * CODE_HIGH) ** (-0.5)

    grad_one = gradient(raw_one, channels)
    grad_two = gradient(raw_two, channels)
    part_one = jnp.sum(grad_one * residue_one, axis=(0, 2))
    part_two = jnp.sum(grad_two * residue_two, axis=(0, 2))
    kept_one = jnp.where(inside_one, grad_one, 0.0).reshape(27, devices, share)
    kept_two = jnp.where(inside_two, grad_two, 0.0).reshape(27, devices, share)
    both = jnp.concatenate([kept_one, kept_two], axis=0).transpose(1, 0, 2)
    both = both.reshape(devices, 54 * share)
    parts = jnp.broadcast_to(
        jnp.concatenate([part_one, part_two])[None], (devices, 2 * channels)
    )
    blocks = jnp.concatenate([both, parts], axis=1)
    blocks = lax.all_to_all(blocks, ("gx", "gy"), 0, 0, tiled=True)
    total = jnp.sum(blocks, axis=0)
    kernels = total[:54 * share].reshape(2, 27, share) * REPORT
    scales = total[54 * share:].reshape(2, channels) * factor
    return (input_grad, kernels[0], scales[0], kernels[1], scales[1])


def solution(mesh):
    in_specs = (P(None, "gx", "gy", None), P(None, "gx", "gy", None), P(), P(), P(), P())
    out_specs = (P(None, "gx", "gy", None), P(None, ("gx", "gy")), P(), P(None, ("gx", "gy")), P())
    return jax.shard_map(
        on_device, mesh=mesh, in_specs=in_specs, out_specs=out_specs, check_vma=False
    )
```

profile of v0, /device:TPU:0, one launch (start us, length us, event | category | flops | bytes accessed | tf_op | source)
XLA Modules:
  0.0 155.2 jit_solution(9966599540901610125)
XLA Ops:
  0.6 1.4 reshape.100
  2.1 0.9 fusion.5
  3.0 1.7 %fusion.8 = bf16[3,3,64,3,64]{4,3,2,1,0:T(4,128)(2,1)} fusion(f32[64]{0:T(128)S(1)} %copy-done.12, f32[3,3,3,64,64]{4,3,2,1,0:T(8,128)S(1)} %reshape.100), kind=kLoop, calls=%fused_computation.28 | loop fusion | flops 552960 | bytes 663808 | tf_op jit(solution)/shard_map/transpose | solution.py:27
  5.0 0.9 fusion.4
  5.9 0.9 fusion.7
  7.6 1.6 %rev.7 = bf16[3,3,3,64,64]{4,1,3,2,0:T(4,128)(2,1)S(1)} reverse(bf16[3,3,3,64,64]{4,1,3,2,0:T(4,128)(2,1)S(1)} %fusion.4), dimensions={0,1,2} | reverse | bytes 442368 | tf_op jit(solution)/shard_map/jit(_flip)/rev | solution.py:34
  9.2 1.0 copy.48
  11.5 1.6 %rev.8 = bf16[3,3,3,64,64]{4,1,3,2,0:T(4,128)(2,1)S(1)} reverse(bf16[3,3,3,64,64]{4,1,3,2,0:T(4,128)(2,1)S(1)} %fusion.5), dimensions={0,1,2} | reverse | bytes 442368 | tf_op jit(solution)/shard_map/jit(_flip)/rev | solution.py:34
  13.1 1.0 copy.49
  15.3 1.7 %broadcast_in_dim.20 = bf16[3,3,64,3,2,64]{5,4,3,2,1,0:T(2,128)(2,1)S(1)} broadcast(bf16[3,3,64,3,64]{4,3,2,1,0:T(4,128)(2,1)} %fusion.8), dimensions={0,1,2,3,5} | broadcast | bytes 663552 | tf_op jit(solution)/shard_map/broadcast_in_dim | solution.py:28
  19.3 1.4 copy_bitcast_fusion.1
  20.8 75.1 %shard_map.101 = (f32[2,8,64,128]{3,2,1,0:T(8,128)S(1)}, f32[3,192,384]{2,1,0:T(8,128)S(1)}, f32[3,192,384]{2,1,0:T(8,128)S(1)}) custom-call(f32[2,8,64,128]{3,2,1,0:T(8,128)S(1)} %get-tuple-element.41.vol, f32[2,8,64,128]{3,2,1,0:T(8,128)S(1)} %get-tuple-element.40.cot, f32[64,128]{1,0:T(8,128)S(1)} %broadcast_in_dim.18.s1, ...), custom_call_target="tpu_custom_call" | custom-call | tf_op jit(solution)/shard_map/pallas_call | solution.py:229
  96.8 2.3 %reshape.107 = f32[3,3,64,3,2,64]{5,4,3,2,1,0:T(2,128)} reshape(f32[3,192,384]{2,1,0:T(8,128)S(1)} %get-tuple-element.9) | data formatting | bytes 1769472 | tf_op jit(solution)/shard_map/reshape | solution.py:213
  99.1 4.0 %reduce_sum.45 = f32[3,3,64,3,64]{4,3,2,1,0:T(4,128)S(1)} reduce(f32[3,3,64,3,2,64]{5,4,3,2,1,0:T(2,128)} %reshape.107, f32[]{:T(128)} %constant.1.clone.1), dimensions={4}, to_apply=%region_0.1 | reduce | flops 110592 | bytes 1327108 | tf_op jit(solution)/shard_map/reduce_sum | solution.py:213
  103.2 1.4 fusion.1
  104.6 2.3 %reshape.110 = f32[3,3,64,3,2,64]{5,4,3,2,1,0:T(2,128)} reshape(f32[3,192,384]{2,1,0:T(8,128)S(1)} %get-tuple-element.10) | data formatting | bytes 1769472 | tf_op jit(solution)/shard_map/reshape | solution.py:213
  106.9 4.0 %reduce_sum.46 = f32[3,3,64,3,64]{4,3,2,1,0:T(4,128)S(1)} reduce(f32[3,3,64,3,2,64]{5,4,3,2,1,0:T(2,128)} %reshape.110, f32[]{:T(128)} %constant.1.clone.1), dimensions={4}, to_apply=%region_1.2 | reduce | flops 110592 | bytes 1327108 | tf_op jit(solution)/shard_map/reduce_sum | solution.py:213
  111.0 1.4 fusion.3
  112.5 0.9 reshape.111
  114.2 0.8 copy-done.8
  115.7 1.9 %copy.53 = f32[32,1,7040]{2,1,0:T(1,128)} copy(f32[32,1,7040]{2,0,1:T(8,128)S(1)} %maximum_bitcast_fusion) | data formatting | bytes 1802240 | tf_op jit(solution)/shard_map/all_to_all | solution.py:269
  117.6 12.8 %all-to-all-start = ((f32[32,1,7040]{2,1,0:T(1,128)}), f32[32,1,7040]{2,1,0:T(1,128)S(1)}, u32[]{:S(2)}, u32[]{:S(2)}) async-start(f32[32,1,7040]{2,1,0:T(1,128)} %copy.53), calls=%async_computation | async-start | bytes 1802240 | tf_op jit(solution)/shard_map/all_to_all | solution.py:269
  130.4 1.1 copy.54
  131.5 22.0 %all-to-all-done = f32[32,1,7040]{2,1,0:T(1,128)S(1)} async-done(((f32[32,1,7040]{2,1,0:T(1,128)}), f32[32,1,7040]{2,1,0:T(1,128)S(1)}, u32[]{:S(2)}, u32[]{:S(2)}) %all-to-all-start) | async-done | bytes 901152 | tf_op jit(solution)/shard_map/all_to_all | solution.py:269
  (62 shorter events, 9.9 us)
Async XLA Ops:
  0.6 1.4 copy-start.12
  2.1 0.9 copy-start.4
  2.1 2.6 %copy-start.6 = (f32[27,4096]{1,0:T(8,128)S(1)}, f32[27,4096]{1,0:T(8,128)}, u32[]{:S(2)}) copy-start(f32[27,4096]{1,0:T(8,128)} %param.10) | copy-start | bytes 1327108
  3.0 2.0 %copy-start.14 = (f32[64]{0:T(128)S(1)}, f32[64]{0:T(128)}, u32[]{:S(2)}) copy-start(f32[64]{0:T(128)} %param.11) | copy-start | bytes 772
  5.0 1.7 %copy-start.2 = (f32[3,3,3,64,64]{4,3,2,1,0:T(8,128)}, f32[3,3,3,64,64]{4,3,2,1,0:T(8,128)S(1)}, u32[]{:S(2)}) copy-start(f32[3,3,3,64,64]{4,3,2,1,0:T(8,128)S(1)} %reshape.102) | copy-start | bytes 1327108
  18.3 1.0 copy-start.10
  96.0 0.8 copy-start
  99.1 4.1 %copy-start.5 = (f32[3,3,3,64,64]{4,3,2,1,0:T(8,128)S(1)}, f32[3,3,3,64,64]{4,3,2,1,0:T(8,128)}, u32[]{:S(2)}) copy-start(f32[3,3,3,64,64]{4,3,2,1,0:T(8,128)} %copy-done.4) | copy-start | bytes 1327108
  99.1 4.1 %copy-start.13 = (f32[64]{0:T(128)S(1)}, f32[64]{0:T(128)}, u32[]{:S(2)}) copy-start(f32[64]{0:T(128)} %param.9) | copy-start | bytes 772
  106.9 4.1 %copy-start.3 = (f32[3,3,3,64,64]{4,3,2,1,0:T(8,128)S(1)}, f32[3,3,3,64,64]{4,3,2,1,0:T(8,128)}, u32[]{:S(2)}) copy-start(f32[3,3,3,64,64]{4,3,2,1,0:T(8,128)} %copy-done.2) | copy-start | bytes 1327108
  106.9 4.1 %copy-start.15 = (f32[64]{0:T(128)S(1)}, f32[64]{0:T(128)}, u32[]{:S(2)}) copy-start(f32[64]{0:T(128)} %param.11) | copy-start | bytes 772
  112.5 1.1 copy-start.7
  112.5 1.1 copy-start.11
  114.0 1.1 copy-start.8
  114.0 1.4 copy-start.9
  117.6 12.8 %copy-start.1 = (f32[2,8,64,128]{3,2,1,0:T(8,128)S(1)}, f32[2,8,64,128]{3,2,1,0:T(8,128)}, u32[]{:S(2)}) copy-start(f32[2,8,64,128]{3,2,1,0:T(8,128)} %copy-done) | copy-start | bytes 1572868
  117.6 35.8 %all-to-all-start = ((f32[32,1,7040]{2,1,0:T(1,128)}), f32[32,1,7040]{2,1,0:T(1,128)S(1)}, u32[]{:S(2)}, u32[]{:S(2)}) async-start(f32[32,1,7040]{2,1,0:T(1,128)} %copy.53), calls=%async_computation | async-start | bytes 1802240 | tf_op jit(solution)/shard_map/all_to_all | solution.py:269
where the time goes:
time: 156 us; the launch traced here: 155 us
  Pallas kernels  75.1 us (48%)
  local copies, waits for them, and re-layouts  28.3 us (18%)
  waiting for transfers between devices  22 us (14%)
  other arithmetic  16 us (10%)
  starting transfers between devices  12.8 us (8%)
    pallas_call x1, Pallas kernels, on_device(): pl.pallas_call(functools.partial(kernel, sizes), out_shape=(cells, grads,...  75.1 us
    all_to_all x1, waiting for transfers between devices, on_device(): blocks = lax.all_to_all(blocks, ('gx', 'gy'), 0, 0, tiled=True)  22 us
    all_to_all x1, starting transfers between devices, on_device(): blocks = lax.all_to_all(blocks, ('gx', 'gy'), 0, 0, tiled=True)  12.8 us
    reduce_sum x2, other arithmetic, gradient(): taps = raw.reshape(3, 3, channels, 3, 2, channels).sum(axis=4)  8.09 us
    reshape x2, local copies, waits for them, and re-layouts, gradient(): taps = raw.reshape(3, 3, channels, 3, 2, channels).sum(axis=4)  4.69 us
    unnamed x35, local copies, waits for them, and re-layouts  3.61 us
    rev x2, local copies, waits for them, and re-layouts, backward_matrix(): jnp.flip(levels.astype(jnp.bfloat16).reshape(3, 3, 3, ch, ch), (0, 1, 2))  3.28 us
  transfers between devices with their start and end apart: 1, of which 1 were waited for; matrix products, arithmetic and copies ran while one was open for 1% of the time, Pallas kernels for 0%

commit v1 on v0

v1 whole, which is shorter than its diff:
```python
import functools

import jax
import jax.numpy as jnp
from jax import lax
from jax.experimental import pallas as pl
from jax.experimental.pallas import tpu as pltpu
from jax.sharding import PartitionSpec as P

CODE_LOW = -8.0
CODE_HIGH = 7.0
REPORT = 2.0 ** (-10)
WAYS = [(dx, dy) for dx in (-1, 0, 1) for dy in (-1, 0, 1) if (dx, dy) != (0, 0)]


def quantize(weight, scale):
    ratio = weight / scale
    level = jnp.clip(jnp.floor(ratio + 0.5), CODE_LOW, CODE_HIGH)
    inside = jnp.logical_and(ratio >= CODE_LOW, ratio <= CODE_HIGH)
    return level, inside, jnp.where(inside, level - ratio, level)


def halves(value):
    high = value.astype(jnp.bfloat16)
    low = (value - high.astype(jnp.float32)).astype(jnp.bfloat16)
    return high, low


def kernel(
    sizes, vol, cot, s1, s2, w1, w2, out, share1, share2,
    pad0, pad1, pad2, pad3, vol_h, hid_h, del_h, stage, slope,
    f1, f2, b2, b1, g1, g2, folded, box1, box2, land1, land2,
    send_sem, recv_sem, out_sem, in_sem,
):
    nx, ny, ch, width = vol.shape
    size_x, size_y = sizes
    me_x, me_y = lax.axis_index("gx"), lax.axis_index("gy")
    devices = size_x * size_y
    me = me_x * size_y + me_y
    group = devices // box1.shape[0]
    lane = lax.broadcasted_iota(jnp.int32, (ch, width), 1)

    for pad in (pad0, pad1, pad2, pad3):
        pad[...] = jnp.zeros_like(pad)

    def there(dx, dy):
        x, y = me_x + dx, me_y + dy
        return (x >= 0) & (x < size_x) & (y >= 0) & (y < size_y)

    barrier = pltpu.get_barrier_semaphore()

    def greet(k, carry):
        other = lax.rem(me + k, devices)
        pl.semaphore_signal(
            barrier, inc=1, device_id=(other // size_y, lax.rem(other, size_y)),
            device_id_type=pl.DeviceIdType.MESH,
        )
        return carry

    lax.fori_loop(1, devices, greet, 0)
    pad0[1:nx + 1, 1:ny + 1] = vol[...]
    pl.semaphore_wait(barrier, devices - 1)

    def spans(step, length):
        if step == 1:
            return pl.ds(length, 1), pl.ds(0, 1)
        if step == -1:
            return pl.ds(1, 1), pl.ds(length + 1, 1)
        return pl.ds(1, length), pl.ds(1, length)

    def remote(pad, turn, way, dx, dy):
        from_x, to_x = spans(dx, nx)
        from_y, to_y = spans(dy, ny)
        return pltpu.make_async_remote_copy(
            src_ref=pad.at[from_x, from_y],
            dst_ref=pad.at[to_x, to_y],
            send_sem=send_sem.at[turn, way],
            recv_sem=recv_sem.at[turn, way],
            device_id=(me_x + dx, me_y + dy),
            device_id_type=pl.DeviceIdType.MESH,
        )

    def send(pad, turn):
        for way, (dx, dy) in enumerate(WAYS):
            @pl.when(there(dx, dy))
            def _(way=way, dx=dx, dy=dy):
                remote(pad, turn, way, dx, dy).start()

    def receive(pad, turn):
        for way, (dx, dy) in enumerate(WAYS):
            @pl.when(there(-dx, -dy))
            def _(way=way, dx=dx, dy=dy):
                remote(pad, turn, way, dx, dy).wait_recv()

    def sent(pad, turn):
        for way, (dx, dy) in enumerate(WAYS):
            @pl.when(there(dx, dy))
            def _(way=way, dx=dx, dy=dy):
                remote(pad, turn, way, dx, dy).wait_send()

    def split(pad, target):
        for x in range(nx + 2):
            def body(y, carry, x=x):
                high, low = halves(pad[x, y])
                target[x, y, 0:ch, :] = high
                target[x, y, ch:2 * ch, :] = low
                return carry

            lax.fori_loop(0, ny + 2, body, 0)

    def matrices(weight, scale, forward, backward):
        for a in range(3):
            for b in range(3):
                for c in range(3):
                    level, _, _ = quantize(weight[9 * a + 3 * b + c], scale[...])
                    flipped = jnp.concatenate([level, level], axis=0).T[0:ch]
                    at = (3 * a + b) * 2 * ch
                    forward[c * ch:(c + 1) * ch, at:at + 2 * ch] = level.astype(jnp.bfloat16)
                    at = (3 * (2 - a) + 2 - b) * 2 * ch
                    backward[(2 - c) * ch:(3 - c) * ch, at:at + 2 * ch] = flipped.astype(
                        jnp.bfloat16
                    )

    def around(source, x, y):
        blocks = []
        for k in (0, 1):
            blocks.append(jnp.concatenate(
                [source[x + a, pl.ds(y + k, 3)].reshape(6 * ch, width) for a in range(3)],
                axis=0,
            ))
        return jnp.concatenate(blocks, axis=1)

    def conv_rows(source, matrix, x, y):
        total = jnp.dot(
            matrix[...], around(source, x, y), preferred_element_type=jnp.float32
        )
        rows = []
        for k in (0, 1):
            part = total[:, k * width:(k + 1) * width]
            before = jnp.where(lane == 0, 0.0, pltpu.roll(part[0:ch], 1, 1))
            after = jnp.where(
                lane == width - 1, 0.0, pltpu.roll(part[2 * ch:3 * ch], width - 1, 1)
            )
            rows.append(before + part[ch:2 * ch] + after)
        return rows

    def grad_rows(source, target, x, y):
        stacks = []
        for k in (0, 1):
            delta = stage[x, y + k]
            left = jnp.where(lane == width - 1, 0.0, pltpu.roll(delta, width - 1, 1))
            right = jnp.where(lane == 0, 0.0, pltpu.roll(delta, 1, 1))
            parts = []
            for shifted in (left, delta, right):
                parts.extend(halves(shifted))
            stacks.append(jnp.concatenate(parts, axis=0))
        prod = lax.dot_general(
            jnp.concatenate(stacks, axis=1), around(source, x, y),
            (((1,), (1,)), ((), ())), preferred_element_type=jnp.float32,
        )
        for c in range(3):
            first = prod[2 * c * ch:(2 * c + 1) * ch]
            second = prod[(2 * c + 1) * ch:(2 * c + 2) * ch]
            target[c * ch:(c + 1) * ch, :] += first + second

    def each_pair(body):
        for x in range(nx):
            def step(j, carry, x=x):
                body(x, 2 * j)
                return carry

            lax.fori_loop(0, ny // 2, step, 0)

    def collect(target, weight, scale, box):
        summed = jnp.zeros((ch, 2 * ch), jnp.float32)
        for a in range(3):
            for b in range(3):
                for c in range(3):
                    tap = 9 * a + 3 * b + c
                    at = (3 * a + b) * 2 * ch
                    value = target[c * ch:(c + 1) * ch, at:at + 2 * ch]
                    value = value + pltpu.roll(value, ch, 1)
                    _, inside, residue = quantize(weight[tap], scale[...])
                    summed = summed + value * residue
                    folded[tap] = jnp.where(inside, value, 0.0)
        line = 0.5 * jnp.sum(jnp.concatenate([summed, summed], axis=0).T, axis=0, keepdims=True)
        half = lax.broadcasted_iota(jnp.int32, (ch // 2, 2 * ch), 1) < ch
        for tap in range(27):
            even = folded[tap, pl.ds(0, ch // 2, stride=2), :]
            odd = folded[tap, pl.ds(1, ch // 2, stride=2), :]
            box[:, tap, :] = jnp.where(half, even, odd)
        box[:, 27, :] = jnp.broadcast_to(line, (ch // 2, 2 * ch))

    def scatter(box, land, turn):
        def one(k, carry):
            other = lax.rem(me + k, devices)
            pltpu.make_async_remote_copy(
                src_ref=box.at[other // group],
                dst_ref=land.at[k],
                send_sem=out_sem.at[turn],
                recv_sem=in_sem.at[turn],
                device_id=(other // size_y, lax.rem(other, size_y)),
                device_id_type=pl.DeviceIdType.MESH,
            ).start()
            return carry

        lax.fori_loop(1, devices, one, 0)
        land[0] = box[me // group]

    def gather(land, turn, share):
        others = land.at[pl.ds(1, devices - 1)]
        pltpu.make_async_copy(others, others, in_sem.at[turn]).wait()

        def add(source, total):
            return total + land[lax.rem(me - source + devices, devices)]

        share[...] = lax.fori_loop(0, devices, add, jnp.zeros(share.shape, jnp.float32))
        pltpu.make_async_copy(others, others, out_sem.at[turn]).wait()

    send(pad0, 0)
    matrices(w1, s1, f1, b1)
    matrices(w2, s2, f2, b2)
    g1[...] = jnp.zeros_like(g1)
    g2[...] = jnp.zeros_like(g2)
    box1[...] = jnp.zeros_like(box1)
    box2[...] = jnp.zeros_like(box2)
    receive(pad0, 0)
    split(pad0, vol_h)

    def first(x, y):
        for k, row in enumerate(conv_rows(vol_h, f1, x, y)):
            pre = row * s1[...]
            sig = 1.0 / (1.0 + jnp.exp(-pre))
            stage[x, y + k] = pre * sig
            slope[x, y + k] = sig * (1.0 + pre * (1.0 - sig))

    each_pair(first)

    pad1[1:nx + 1, 1:ny + 1] = stage[...]
    send(pad1, 1)
    receive(pad1, 1)
    split(pad1, hid_h)

    def second(x, y):
        for k, row in enumerate(conv_rows(hid_h, f2, x, y)):
            pre = row * s2[...]
            sig = 1.0 / (1.0 + jnp.exp(-pre))
            stage[x, y + k] = cot[x, y + k] * (sig * (1.0 + pre * (1.0 - sig)))

    each_pair(second)

    pad2[1:nx + 1, 1:ny + 1] = stage[...] * s2[...]
    send(pad2, 2)
    each_pair(lambda x, y: grad_rows(hid_h, g2, x, y))
    collect(g2, w2, s2, box2)
    scatter(box2, land2, 1)
    receive(pad2, 2)
    split(pad2, del_h)

    def third(x, y):
        for k, row in enumerate(conv_rows(del_h, b2, x, y)):
            stage[x, y + k] = row * slope[x, y + k]

    each_pair(third)

    pad3[1:nx + 1, 1:ny + 1] = stage[...] * s1[...]
    send(pad3, 3)
    each_pair(lambda x, y: grad_rows(vol_h, g1, x, y))
    collect(g1, w1, s1, box1)
    scatter(box1, land1, 0)
    receive(pad3, 3)
    split(pad3, del_h)

    def fourth(x, y):
        for k, row in enumerate(conv_rows(del_h, b1, x, y)):
            out[x, y + k] = row

    each_pair(fourth)
    gather(land2, 1, share2)
    gather(land1, 0, share1)
    for turn, pad in enumerate((pad0, pad1, pad2, pad3)):
        sent(pad, turn)


def on_device(volume, cotangent, weight_one, scale_one, weight_two, scale_two):
    channels = scale_one.shape[0]
    ch, nx, ny, width = volume.shape
    sizes = (lax.axis_size("gx"), lax.axis_size("gy"))
    devices = sizes[0] * sizes[1]
    vmem = pl.BlockSpec(memory_space=pltpu.VMEM)
    cells = jax.ShapeDtypeStruct((nx, ny, ch, width), jnp.float32)
    block = jax.ShapeDtypeStruct((32, 2 * ch), jnp.float32)
    pad = pltpu.VMEM((nx + 2, ny + 2, ch, width), jnp.float32)
    half = pltpu.VMEM((nx + 2, ny + 2, 2 * ch, width), jnp.bfloat16)
    local = pltpu.VMEM((nx, ny, ch, width), jnp.float32)
    matrix = pltpu.VMEM((3 * ch, 18 * ch), jnp.bfloat16)
    grads = pltpu.VMEM((3 * ch, 18 * ch), jnp.float32)
    box = pltpu.VMEM((ch // 2, 32, 2 * ch), jnp.float32)
    land = pltpu.VMEM((devices, 32, 2 * ch), jnp.float32)

    def twice(weight):
        taps = weight.reshape(27, ch, ch)
        return jnp.concatenate([taps, taps], axis=2)

    moved, block_one, block_two = pl.pallas_call(
        functools.partial(kernel, sizes),
        out_shape=(cells, block, block),
        in_specs=[vmem] * 6,
        out_specs=(vmem, vmem, vmem),
        scratch_shapes=[
            pad, pad, pad, pad, half, half, half, local, local,
            matrix, matrix, matrix, matrix, grads, grads,
            pltpu.VMEM((27, ch, 2 * ch), jnp.float32), box, box, land, land,
            pltpu.SemaphoreType.DMA((4, 8)),
            pltpu.SemaphoreType.DMA((4, 8)),
            pltpu.SemaphoreType.DMA((2,)),
            pltpu.SemaphoreType.DMA((2,)),
        ],
        compiler_params=pltpu.CompilerParams(
            collective_id=0, has_side_effects=True, vmem_limit_bytes=52 * 2 ** 20
        ),
    )(
        volume.transpose(1, 2, 0, 3),
        cotangent.transpose(1, 2, 0, 3),
        jnp.broadcast_to(scale_one[:, None], (ch, width)),
        jnp.broadcast_to(scale_two[:, None], (ch, width)),
        twice(weight_one),
        twice(weight_two),
    )
    input_grad = moved.transpose(2, 0, 1, 3)
    share = channels * channels // devices
    group = 2 * ch // share
    first_col = lax.rem(lax.axis_index(("gx", "gy")), group) * share
    factor = REPORT * (27.0 * channels * CODE_HIGH) ** (-0.5)

    def results(block):
        kernels = lax.dynamic_slice(block, (0, first_col), (27, share)) * REPORT
        return kernels, block[27, :channels] * factor

    kernel_one, scales_one = results(block_one)
    kernel_two, scales_two = results(block_two)
    return (input_grad, kernel_one, scales_one, kernel_two, scales_two)


def solution(mesh):
    in_specs = (P(None, "gx", "gy", None), P(None, "gx", "gy", None), P(), P(), P(), P())
    out_specs = (P(None, "gx", "gy", None), P(None, ("gx", "gy")), P(), P(None, ("gx", "gy")), P())
    return jax.shard_map(
        on_device, mesh=mesh, in_specs=in_specs, out_specs=out_specs, check_vma=False
    )
```

time: 156 us -> 99.4 us (0.64)
  local copies, waits for them, and re-layouts: 28.3 us -> 5.43 us
  waiting for transfers between devices: 22 us -> 0 us
  Pallas kernels: 75.1 us -> 88.4 us
  starting transfers between devices: 12.8 us -> 0 us
  other arithmetic: 16 us -> 3.59 us
    all_to_all x1 -> x0, waiting for transfers between devices: 22 us -> none  [on_device(): blocks = lax.all_to_all(blocks, ('gx', 'gy'), 0, 0, tiled=True)]
    pallas_call x1, Pallas kernels: 75.1 us -> 88.4 us  [on_device(): pl.pallas_call(functools.partial(kernel, sizes), out_shape=(cells, block,...]
    all_to_all x1 -> x0, starting transfers between devices: 12.8 us -> none  [on_device(): blocks = lax.all_to_all(blocks, ('gx', 'gy'), 0, 0, tiled=True)]
    reduce_sum x5 -> x0, other arithmetic: 11.4 us -> none  [the longest x2 8.09 us: gradient(): taps = raw.reshape(3, 3, channels, 3, 2, channels).sum(axis=4)]
    reshape x10 -> x2, local copies, waits for them, and re-layouts: 9.67 us -> 1.73 us  [twice(): taps = weight.reshape(27, ch, ch)]
    broadcast_in_dim x4 -> x0, local copies, waits for them, and re-layouts: 3.71 us -> none  [the longest x2 2.4 us: forward_matrix(): taps = jnp.broadcast_to(taps[:, :, :, :, None, :], (3, 3, ch, 3, 2, ch))]
    transpose x5 -> x0, local copies, waits for them, and re-layouts: 3.61 us -> none  [the longest x2 2.06 us: backward_matrix(): taps = taps.transpose(0, 2, 4, 1, 3)]
    rev x2 -> x0, local copies, waits for them, and re-layouts: 3.28 us -> none  [backward_matrix(): jnp.flip(levels.astype(jnp.bfloat16).reshape(3, 3, 3, ch, ch), (0, 1, 2))]
  transfers between devices with their start and end apart: 1 -> 0, of which waited for: 1 -> 0; matrix products, arithmetic and copies ran while one was open for 1% -> 0% of each run, Pallas kernels for 0% -> 0%
where the time goes in v1:
time: 99.4 us; the launch traced here: 98.1 us
  Pallas kernels  88.4 us (89%)
  local copies, waits for them, and re-layouts  5.43 us (5%)
  other arithmetic  3.59 us (4%)
    pallas_call x1, Pallas kernels, on_device(): pl.pallas_call(functools.partial(kernel, sizes), out_shape=(cells, block,...  88.4 us
    unnamed x13, local copies, waits for them, and re-layouts  3.56 us
    concatenate x2, other arithmetic, twice(): return jnp.concatenate([taps, taps], axis=2)  2.46 us

profile of v1, /device:TPU:0, one launch (start us, length us, event | category | flops | bytes accessed | tf_op | source)
XLA Modules:
  0.0 98.1 jit_solution(16388825457553096947)
XLA Ops:
  0.6 1.4 %reshape.22 = f32[27,64,64]{2,1,0:T(8,128)S(1)} reshape(f32[27,4096]{1,0:T(8,128)} %param.8) | data formatting | bytes 884736 | tf_op jit(solution)/shard_map/reshape | solution.py:302
  2.0 0.0 copy-start.2
  2.0 1.2 %pad_maximum_fusion.w1 = f32[27,64,128]{2,1,0:T(8,128)} fusion(f32[27,64,64]{2,1,0:T(8,128)S(1)} %reshape.22), kind=kLoop, calls=%fused_computation | loop fusion | flops 221184 | bytes 1327104 | tf_op jit(solution)/shard_map/concatenate | solution.py:303
  3.3 0.0 copy-done.2
  3.3 0.3 reshape.23
  3.6 0.0 copy-start
  3.6 1.2 %pad_maximum_fusion.1.w2 = f32[27,64,128]{2,1,0:T(8,128)} fusion(f32[27,64,64]{2,1,0:T(8,128)S(1)} %reshape.23), kind=kLoop, calls=%fused_computation.1 | loop fusion | flops 221184 | bytes 1327104 | tf_op jit(solution)/shard_map/concatenate | solution.py:303
  4.9 0.0 copy-done
  4.9 0.0 copy-start.1
  4.9 0.2 copy.17
  5.0 0.9 copy-done.1
  5.9 0.2 copy.16
  6.1 0.0 copy-start.3
  6.1 0.6 copy-done.3
  6.7 0.0 copy-start.4
  6.7 0.1 broadcast_in_dim.4.s1
  6.8 0.6 copy-done.4
  7.4 0.1 broadcast_in_dim.5.s2
  7.5 88.4 %shard_map.101 = (f32[2,8,64,128]{3,2,1,0:T(8,128)S(1)}, f32[32,128]{1,0:T(8,128)S(1)}, f32[32,128]{1,0:T(8,128)S(1)}) custom-call(f32[2,8,64,128]{3,2,1,0:T(8,128)S(1)} %bitcast.11, f32[2,8,64,128]{3,2,1,0:T(8,128)S(1)} %bitcast.12, f32[64,128]{1,0:T(8,128)S(1)} %broadcast_in_dim.4.s1, f32[64,128]{1,0:T(8,128)S(1)} %broadcast_in_dim.5.s2, ...), custom_call_target="tpu_custom_call" | custom-call | tf_op jit(solution)/shard_map/pallas_call | solution.py:305
  95.9 0.5 multiply_bitcast_fusion
  96.4 0.6 slice_multiply_fusion
  97.0 1.1 %copy.13 = f32[64,2,8,128]{3,2,1,0:T(8,128)} copy(f32[64,2,8,128]{3,0,2,1:T(8,128)S(1)} %bitcast.13) | data formatting | bytes 1048576
Async XLA Ops:
  2.0 1.2 %copy-start.2 = (f32[27,4096]{1,0:T(8,128)S(1)}, f32[27,4096]{1,0:T(8,128)}, u32[]{:S(2)}) copy-start(f32[27,4096]{1,0:T(8,128)} %param.10) | copy-start | bytes 1327108
  3.6 1.2 %copy-start = (f32[64,2,8,128]{3,2,1,0:T(8,128)S(1)}, f32[64,2,8,128]{3,2,1,0:T(8,128)}, u32[]{:S(2)}) copy-start(f32[64,2,8,128]{3,2,1,0:T(8,128)} %param.6) | copy-start | bytes 1572868
  4.9 1.0 %copy-start.1 = (f32[64,2,8,128]{3,2,1,0:T(8,128)S(1)}, f32[64,2,8,128]{3,2,1,0:T(8,128)}, u32[]{:S(2)}) copy-start(f32[64,2,8,128]{3,2,1,0:T(8,128)} %param.7) | copy-start | bytes 1572868
  6.1 0.7 copy-start.3
  6.7 0.7 copy-start.4

commit v2 on v1

--- a/solution.py
+++ b/solution.py
@@ -108,18 +108,30 @@
 
             lax.fori_loop(0, ny + 2, body, 0)
 
-    def matrices(weight, scale, forward, backward):
-        for a in range(3):
-            for b in range(3):
-                for c in range(3):
-                    level, _, _ = quantize(weight[9 * a + 3 * b + c], scale[...])
-                    flipped = jnp.concatenate([level, level], axis=0).T[0:ch]
-                    at = (3 * a + b) * 2 * ch
-                    forward[c * ch:(c + 1) * ch, at:at + 2 * ch] = level.astype(jnp.bfloat16)
-                    at = (3 * (2 - a) + 2 - b) * 2 * ch
-                    backward[(2 - c) * ch:(3 - c) * ch, at:at + 2 * ch] = flipped.astype(
-                        jnp.bfloat16
-                    )
+    def doubled(weight, tap):
+        value = weight[tap]
+        return jnp.concatenate([value, value], axis=1)
+
+    def tap_place(a, b, c):
+        at = (3 * a + b) * 2 * ch
+        return slice(c * ch, (c + 1) * ch), slice(at, at + 2 * ch)
+
+    taps = [(a, b, c) for a in range(3) for b in range(3) for c in range(3)]
+
+    def forward_matrix(weight, scale, forward):
+        for tap, (a, b, c) in enumerate(taps):
+            level, _, _ = quantize(doubled(weight, tap), scale[...])
+            forward[tap_place(a, b, c)] = level.astype(jnp.bfloat16)
+
+    def backward_matrix(forward, backward):
+        low_lanes = lane < ch
+        for first in range(0, 27, 2):
+            some = taps[first:first + 2]
+            values = [forward[tap_place(*tap)].astype(jnp.float32) for tap in some]
+            mixed = jnp.where(low_lanes, values[0], values[-1])
+            turned = jnp.concatenate([mixed, mixed], axis=0).T.astype(jnp.bfloat16)
+            for k, (a, b, c) in enumerate(some):
+                backward[tap_place(2 - a, 2 - b, 2 - c)] = turned[k * ch:(k + 1) * ch]
 
     def around(source, x, y):
         blocks = []
@@ -164,12 +176,15 @@
             target[c * ch:(c + 1) * ch, :] += first + second
 
     def each_pair(body):
+        pairs = ny // 2
+        joined = 2 if pairs % 2 == 0 else 1
         for x in range(nx):
             def step(j, carry, x=x):
-                body(x, 2 * j)
+                for k in range(joined):
+                    body(x, 2 * (j * joined + k))
                 return carry
 
-            lax.fori_loop(0, ny // 2, step, 0)
+            lax.fori_loop(0, pairs // joined, step, 0)
 
     def collect(target, weight, scale, box):
         summed = jnp.zeros((ch, 2 * ch), jnp.float32)
@@ -180,7 +195,7 @@
                     at = (3 * a + b) * 2 * ch
                     value = target[c * ch:(c + 1) * ch, at:at + 2 * ch]
                     value = value + pltpu.roll(value, ch, 1)
-                    _, inside, residue = quantize(weight[tap], scale[...])
+                    _, inside, residue = quantize(doubled(weight, tap), scale[...])
                     summed = summed + value * residue
                     folded[tap] = jnp.where(inside, value, 0.0)
         line = 0.5 * jnp.sum(jnp.concatenate([summed, summed], axis=0).T, axis=0, keepdims=True)
@@ -218,8 +233,8 @@
         pltpu.make_async_copy(others, others, out_sem.at[turn]).wait()
 
     send(pad0, 0)
-    matrices(w1, s1, f1, b1)
-    matrices(w2, s2, f2, b2)
+    forward_matrix(w1, s1, f1)
+    forward_matrix(w2, s2, f2)
     g1[...] = jnp.zeros_like(g1)
     g2[...] = jnp.zeros_like(g2)
     box1[...] = jnp.zeros_like(box1)
@@ -238,6 +253,8 @@
 
     pad1[1:nx + 1, 1:ny + 1] = stage[...]
     send(pad1, 1)
+    backward_matrix(f2, b2)
+    backward_matrix(f1, b1)
     receive(pad1, 1)
     split(pad1, hid_h)
 
@@ -297,10 +314,6 @@
     grads = pltpu.VMEM((3 * ch, 18 * ch), jnp.float32)
     box = pltpu.VMEM((ch // 2, 32, 2 * ch), jnp.float32)
     land = pltpu.VMEM((devices, 32, 2 * ch), jnp.float32)
-
-    def twice(weight):
-        taps = weight.reshape(27, ch, ch)
-        return jnp.concatenate([taps, taps], axis=2)
 
     moved, block_one, block_two = pl.pallas_call(
         functools.partial(kernel, sizes),
@@ -324,8 +337,8 @@
         cotangent.transpose(1, 2, 0, 3),
         jnp.broadcast_to(scale_one[:, None], (ch, width)),
         jnp.broadcast_to(scale_two[:, None], (ch, width)),
-        twice(weight_one),
-        twice(weight_two),
+        weight_one.reshape(27, ch, ch),
+        weight_two.reshape(27, ch, ch),
     )
     input_grad = moved.transpose(2, 0, 1, 3)
     share = channels * channels // devices

time: 99.4 us -> 95.6 us (0.962)
  the two profiles are of different devices: /device:TPU:0 before, /device:TPU:11 now
where the time goes in v2:
time: 95.6 us; the launch traced here: 95.4 us
  Pallas kernels  86.8 us (91%)
  local copies, waits for them, and re-layouts  6.79 us (7%)
  other arithmetic  1.13 us (1%)
    pallas_call x1, Pallas kernels, on_device(): pl.pallas_call(functools.partial(kernel, sizes), out_shape=(cells, block,...  86.8 us
    unnamed x11, local copies, waits for them, and re-layouts  3.42 us

profile of v2, /device:TPU:11, one launch (start us, length us, event | category | flops | bytes accessed | tf_op | source)
XLA Modules:
  0.0 95.4 jit_solution(4069898128546413234)
XLA Ops:
  0.6 0.0 copy-start.3
  0.6 0.7 broadcast_in_dim.4.s1
  1.4 0.0 copy-done.3
  1.4 0.1 broadcast_in_dim.5.s2
  1.4 0.0 copy-start
  1.4 1.3 %copy.17 = f32[64,2,8,128]{3,0,2,1:T(8,128)S(1)} copy(f32[64,2,8,128]{3,2,1,0:T(8,128)} %param.6) | data formatting | bytes 1048576 | tf_op args[0]
  2.7 0.0 copy-done
  2.7 0.0 copy-start.1
  2.8 0.2 copy.16
  2.9 0.9 copy-done.1
  3.8 0.0 copy-start.2
  3.8 1.3 %reshape.22.w1 = f32[27,64,64]{2,1,0:T(8,128)} reshape(f32[27,4096]{1,0:T(8,128)S(1)} %copy-done.1) | data formatting | bytes 884736 | tf_op jit(solution)/shard_map/reshape | solution.py:340
  5.1 0.0 copy-done.2
  5.1 1.3 %reshape.23.w2 = f32[27,64,64]{2,1,0:T(8,128)} reshape(f32[27,4096]{1,0:T(8,128)S(1)} %copy-done.2) | data formatting | bytes 884736 | tf_op jit(solution)/shard_map/reshape | solution.py:341
  6.4 86.8 %shard_map.101 = (f32[2,8,64,128]{3,2,1,0:T(8,128)S(1)}, f32[32,128]{1,0:T(8,128)S(1)}, f32[32,128]{1,0:T(8,128)S(1)}) custom-call(f32[2,8,64,128]{3,2,1,0:T(8,128)S(1)} %bitcast.11, f32[2,8,64,128]{3,2,1,0:T(8,128)S(1)} %bitcast.12, f32[64,128]{1,0:T(8,128)S(1)} %broadcast_in_dim.4.s1, f32[64,128]{1,0:T(8,128)S(1)} %broadcast_in_dim.5.s2, ...), custom_call_target="tpu_custom_call" | custom-call | tf_op jit(solution)/shard_map/pallas_call | solution.py:318
  93.1 1.1 %copy.13 = f32[64,2,8,128]{3,2,1,0:T(8,128)} copy(f32[64,2,8,128]{3,0,2,1:T(8,128)S(1)} %bitcast.13) | data formatting | bytes 1048576
  94.2 0.5 multiply_bitcast_fusion
  94.8 0.6 slice_multiply_fusion
Async XLA Ops:
  0.6 0.7 copy-start.3
  1.4 1.3 %copy-start = (f32[64,2,8,128]{3,2,1,0:T(8,128)S(1)}, f32[64,2,8,128]{3,2,1,0:T(8,128)}, u32[]{:S(2)}) copy-start(f32[64,2,8,128]{3,2,1,0:T(8,128)} %param.7) | copy-start | bytes 1572868
  2.7 1.0 %copy-start.1 = (f32[27,4096]{1,0:T(8,128)S(1)}, f32[27,4096]{1,0:T(8,128)}, u32[]{:S(2)}) copy-start(f32[27,4096]{1,0:T(8,128)} %param.8) | copy-start | bytes 1327108
  3.8 1.3 %copy-start.2 = (f32[27,4096]{1,0:T(8,128)S(1)}, f32[27,4096]{1,0:T(8,128)}, u32[]{:S(2)}) copy-start(f32[27,4096]{1,0:T(8,128)} %param.10) | copy-start | bytes 1327108

commit v3 on v2

--- a/solution.py
+++ b/solution.py
@@ -30,14 +30,19 @@
     sizes, vol, cot, s1, s2, w1, w2, out, share1, share2,
     pad0, pad1, pad2, pad3, vol_h, hid_h, del_h, stage, slope,
     f1, f2, b2, b1, g1, g2, folded, box1, box2, land1, land2,
-    send_sem, recv_sem, out_sem, in_sem,
+    swap1, swap2, merged1, merged2,
+    send_sem, recv_sem, out_sem, in_sem, pass_sem, take_sem,
 ):
     nx, ny, ch, width = vol.shape
     size_x, size_y = sizes
     me_x, me_y = lax.axis_index("gx"), lax.axis_index("gy")
     devices = size_x * size_y
     me = me_x * size_y + me_y
-    group = devices // box1.shape[0]
+    chips = devices // 2
+    core = lax.rem(me, 2)
+    chip = me // 2
+    sets, boxes = box1.shape[0], box1.shape[1]
+    owners = devices // boxes
     lane = lax.broadcasted_iota(jnp.int32, (ch, width), 1)
 
     for pad in (pad0, pad1, pad2, pad3):
@@ -199,18 +204,32 @@
                     summed = summed + value * residue
                     folded[tap] = jnp.where(inside, value, 0.0)
         line = 0.5 * jnp.sum(jnp.concatenate([summed, summed], axis=0).T, axis=0, keepdims=True)
-        half = lax.broadcasted_iota(jnp.int32, (ch // 2, 2 * ch), 1) < ch
-        for tap in range(27):
-            even = folded[tap, pl.ds(0, ch // 2, stride=2), :]
-            odd = folded[tap, pl.ds(1, ch // 2, stride=2), :]
-            box[:, tap, :] = jnp.where(half, even, odd)
-        box[:, 27, :] = jnp.broadcast_to(line, (ch // 2, 2 * ch))
-
-    def scatter(box, land, turn):
+        half = lax.broadcasted_iota(jnp.int32, (boxes, 2 * ch), 1) < ch
+        for k in range(sets):
+            for tap in range(27):
+                even = folded[tap, pl.ds(2 * k, boxes, stride=2 * sets), :]
+                odd = folded[tap, pl.ds(2 * k + 1, boxes, stride=2 * sets), :]
+                box[k, :, tap, :] = jnp.where(half, even, odd)
+            box[k, :, 27, :] = jnp.broadcast_to(line, (boxes, 2 * ch))
+
+    def exchange(box, swap, turn):
+        return pltpu.make_async_remote_copy(
+            src_ref=box.at[lax.rem(1 - core, sets)],
+            dst_ref=swap,
+            send_sem=pass_sem.at[turn],
+            recv_sem=take_sem.at[turn],
+            device_id=(me_x, me_y + 1 - 2 * core),
+            device_id_type=pl.DeviceIdType.MESH,
+        )
+
+    def scatter(box, swap, merged, land, turn):
+        exchange(box, swap, turn).wait_recv()
+        merged[...] = box[lax.rem(core, sets)] + swap[...]
+
         def one(k, carry):
-            other = lax.rem(me + k, devices)
+            other = 2 * lax.rem(chip + k, chips) + core
             pltpu.make_async_remote_copy(
-                src_ref=box.at[other // group],
+                src_ref=merged.at[other // owners],
                 dst_ref=land.at[k],
                 send_sem=out_sem.at[turn],
                 recv_sem=in_sem.at[turn],
@@ -219,17 +238,17 @@
             ).start()
             return carry
 
-        lax.fori_loop(1, devices, one, 0)
-        land[0] = box[me // group]
+        lax.fori_loop(1, chips, one, 0)
+        land[0] = merged[me // owners]
 
     def gather(land, turn, share):
-        others = land.at[pl.ds(1, devices - 1)]
+        others = land.at[pl.ds(1, chips - 1)]
         pltpu.make_async_copy(others, others, in_sem.at[turn]).wait()
 
         def add(source, total):
-            return total + land[lax.rem(me - source + devices, devices)]
-
-        share[...] = lax.fori_loop(0, devices, add, jnp.zeros(share.shape, jnp.float32))
+            return total + land[lax.rem(chip - source + chips, chips)]
+
+        share[...] = lax.fori_loop(0, chips, add, jnp.zeros(share.shape, jnp.float32))
         pltpu.make_async_copy(others, others, out_sem.at[turn]).wait()
 
     send(pad0, 0)
@@ -270,9 +289,10 @@
     send(pad2, 2)
     each_pair(lambda x, y: grad_rows(hid_h, g2, x, y))
     collect(g2, w2, s2, box2)
-    scatter(box2, land2, 1)
+    exchange(box2, swap2, 1).start()
     receive(pad2, 2)
     split(pad2, del_h)
+    scatter(box2, swap2, merged2, land2, 1)
 
     def third(x, y):
         for k, row in enumerate(conv_rows(del_h, b2, x, y)):
@@ -284,9 +304,10 @@
     send(pad3, 3)
     each_pair(lambda x, y: grad_rows(vol_h, g1, x, y))
     collect(g1, w1, s1, box1)
-    scatter(box1, land1, 0)
+    exchange(box1, swap1, 0).start()
     receive(pad3, 3)
     split(pad3, del_h)
+    scatter(box1, swap1, merged1, land1, 0)
 
     def fourth(x, y):
         for k, row in enumerate(conv_rows(del_h, b1, x, y)):
@@ -297,6 +318,8 @@
     gather(land1, 0, share1)
     for turn, pad in enumerate((pad0, pad1, pad2, pad3)):
         sent(pad, turn)
+    exchange(box1, swap1, 0).wait_send()
+    exchange(box2, swap2, 1).wait_send()
 
 
 def on_device(volume, cotangent, weight_one, scale_one, weight_two, scale_two):
@@ -312,8 +335,11 @@
     local = pltpu.VMEM((nx, ny, ch, width), jnp.float32)
     matrix = pltpu.VMEM((3 * ch, 18 * ch), jnp.bfloat16)
     grads = pltpu.VMEM((3 * ch, 18 * ch), jnp.float32)
-    box = pltpu.VMEM((ch // 2, 32, 2 * ch), jnp.float32)
-    land = pltpu.VMEM((devices, 32, 2 * ch), jnp.float32)
+    sets = 2 if devices == ch // 2 else 1
+    boxes = ch // 2 // sets
+    box = pltpu.VMEM((sets, boxes, 32, 2 * ch), jnp.float32)
+    part = pltpu.VMEM((boxes, 32, 2 * ch), jnp.float32)
+    land = pltpu.VMEM((devices // 2, 32, 2 * ch), jnp.float32)
 
     moved, block_one, block_two = pl.pallas_call(
         functools.partial(kernel, sizes),
@@ -324,8 +350,11 @@
             pad, pad, pad, pad, half, half, half, local, local,
             matrix, matrix, matrix, matrix, grads, grads,
             pltpu.VMEM((27, ch, 2 * ch), jnp.float32), box, box, land, land,
+            part, part, part, part,
             pltpu.SemaphoreType.DMA((4, 8)),
             pltpu.SemaphoreType.DMA((4, 8)),
+            pltpu.SemaphoreType.DMA((2,)),
+            pltpu.SemaphoreType.DMA((2,)),
             pltpu.SemaphoreType.DMA((2,)),
             pltpu.SemaphoreType.DMA((2,)),
         ],

time: 95.6 us -> 95.7 us (level)
  the two profiles are of different devices: /device:TPU:11 before, /device:TPU:0 now
where the time goes in v3:
time: 95.7 us; the launch traced here: 95.5 us
  Pallas kernels  86.9 us (91%)
  local copies, waits for them, and re-layouts  6.79 us (7%)
  other arithmetic  1.13 us (1%)
    pallas_call x1, Pallas kernels, on_device(): pl.pallas_call(functools.partial(kernel, sizes), out_shape=(cells, block,...  86.9 us
    unnamed x11, local copies, waits for them, and re-layouts  3.42 us

profile of v3, /device:TPU:0, one launch (start us, length us, event | category | flops | bytes accessed | tf_op | source)
XLA Modules:
  0.0 95.5 jit_solution(9075058622431117048)
XLA Ops:
  0.6 0.0 copy-start.3
  0.6 0.7 broadcast_in_dim.4.s1
  1.4 0.0 copy-done.3
  1.4 0.1 broadcast_in_dim.5.s2
  1.4 0.0 copy-start
  1.4 1.3 %copy.17 = f32[64,2,8,128]{3,0,2,1:T(8,128)S(1)} copy(f32[64,2,8,128]{3,2,1,0:T(8,128)} %param.6) | data formatting | bytes 1048576 | tf_op args[0]
  2.7 0.0 copy-done
  2.7 0.0 copy-start.1
  2.8 0.2 copy.16
  2.9 0.9 copy-done.1
  3.8 0.0 copy-start.2
  3.8 1.3 %reshape.22.w1 = f32[27,64,64]{2,1,0:T(8,128)} reshape(f32[27,4096]{1,0:T(8,128)S(1)} %copy-done.1) | data formatting | bytes 884736 | tf_op jit(solution)/shard_map/reshape | solution.py:369
  5.1 0.0 copy-done.2
  5.1 1.3 %reshape.23.w2 = f32[27,64,64]{2,1,0:T(8,128)} reshape(f32[27,4096]{1,0:T(8,128)S(1)} %copy-done.2) | data formatting | bytes 884736 | tf_op jit(solution)/shard_map/reshape | solution.py:370
  6.4 86.9 %shard_map.101 = (f32[2,8,64,128]{3,2,1,0:T(8,128)S(1)}, f32[32,128]{1,0:T(8,128)S(1)}, f32[32,128]{1,0:T(8,128)S(1)}) custom-call(f32[2,8,64,128]{3,2,1,0:T(8,128)S(1)} %bitcast.11, f32[2,8,64,128]{3,2,1,0:T(8,128)S(1)} %bitcast.12, f32[64,128]{1,0:T(8,128)S(1)} %broadcast_in_dim.4.s1, f32[64,128]{1,0:T(8,128)S(1)} %broadcast_in_dim.5.s2, ...), custom_call_target="tpu_custom_call" | custom-call | tf_op jit(solution)/shard_map/pallas_call | solution.py:344
  93.3 1.1 %copy.13 = f32[64,2,8,128]{3,2,1,0:T(8,128)} copy(f32[64,2,8,128]{3,0,2,1:T(8,128)S(1)} %bitcast.13) | data formatting | bytes 1048576
  94.4 0.5 multiply_bitcast_fusion
  94.9 0.6 slice_multiply_fusion
Async XLA Ops:
  0.6 0.7 copy-start.3
  1.4 1.3 %copy-start = (f32[64,2,8,128]{3,2,1,0:T(8,128)S(1)}, f32[64,2,8,128]{3,2,1,0:T(8,128)}, u32[]{:S(2)}) copy-start(f32[64,2,8,128]{3,2,1,0:T(8,128)} %param.7) | copy-start | bytes 1572868
  2.7 1.0 %copy-start.1 = (f32[27,4096]{1,0:T(8,128)S(1)}, f32[27,4096]{1,0:T(8,128)}, u32[]{:S(2)}) copy-start(f32[27,4096]{1,0:T(8,128)} %param.8) | copy-start | bytes 1327108
  3.8 1.3 %copy-start.2 = (f32[27,4096]{1,0:T(8,128)S(1)}, f32[27,4096]{1,0:T(8,128)}, u32[]{:S(2)}) copy-start(f32[27,4096]{1,0:T(8,128)} %param.10) | copy-start | bytes 1327108
